TPU v7x, 32 devices: a whole 2x2x4 slice. The times are simulated.
32 devices in a mesh: grp: 2 (over y), pan: 4 (over z), en: 4 (over x, core).
Axes of the slice: x: 2, y: 2, z: 4, core: 2. Of those that a mesh axis runs over, the one named last changes fastest.
Arguments:
- retarded: float32 [2, 8, 2048, 2048], P(None, ('grp', 'en'), 'pan'), parts along dimension 1, may hold values from -0.75 to 0.75
- contact: float32 [2, 8, 2048, 128], P(None, ('grp', 'en'), 'pan'), parts along dimension 1, may hold values from -6 to 6
- atom_kind: int32 [256], replicated, may hold values from 0 to 3
- coupling: float32 [4, 3], replicated, may hold values from 0.2 to 1
- shifts: int32 [3], replicated, may hold values from 1 to 3, as said below
Outputs:
- lesser_diag: float32 [2, 8, 2048, 128], P(None, ('grp', 'en'), 'pan'), parts along dimension 1
- lesser_upper: float32 [2, 8, 2048, 128], P(None, ('grp', 'en'), 'pan'), parts along dimension 1
- sigma_next: float32 [2, 8, 2048, 128], P(None, ('grp', 'en'), 'pan'), parts along dimension 1
There are 2 independent parts, one for each index of `grp`. A program takes and returns all parts, laid end to end along the dimension named above; an argument that names none is the same for every part. Nothing has to cross between parts.
Inputs may be any that keep to these rules, and one draw needn't show every extreme that they name: `shifts`: the three entries are distinct: one is 1, one is 3, and one lies strictly between them.
All inputs are finite; a program needn't handle non-finite values.
Results may differ from a plain program's by a relative error of at most 0.0001.
Values sent between devices are 32-bit elements; how exact they have to be, the bound alone decides.
A program may use at most 128 MiB of HBM per device.

v0:
```python
import functools
import math

import jax
import jax.numpy as jnp
from jax import lax
from jax.experimental import pallas as pl
from jax.experimental.pallas import tpu as pltpu
from jax.sharding import PartitionSpec as P

B = 128
ORB = 8
ITERS = 2
MESH = pl.DeviceIdType.MESH


def split(x):
    hi = x.astype(jnp.bfloat16)
    return hi, (x - hi.astype(jnp.float32)).astype(jnp.bfloat16)


def nn(a, b):
    return jnp.dot(a, b, preferred_element_type=jnp.float32)


def nt(a, b):
    return lax.dot_general(a, b, (((1,), (1,)), ((), ())), preferred_element_type=jnp.float32)


def three(f, a, b):
    return f(a[0], b[0]) + (f(a[1], b[0]) + f(a[0], b[1]))


def kernel(
    n, energies, L, modes,
    green, contact, ccol, crow, shifts,
    diag_out, upper_out, sigma_out,
    gst, rhi, rlo, zbuf, gnext, gprev, dacc, uacc, uret, uadd, dbuf, sib, xsend, xrecv,
    gsem, zs, zr, ns, nr, ps, pr, us, ur, ss, sr, xs, xr,
):
    NB = n * L
    rows = L * B
    X = energies // 2
    scale = 1.0 / math.sqrt(B)
    z = lax.axis_index("pan")
    e = lax.axis_index("en")
    x = lax.div(e, 2)
    core = lax.rem(e, 2)
    other = x * 2 + 1 - core

    load = pltpu.make_async_copy(green.at[:, 0], gst, gsem)
    load.start()
    zbuf[0, pl.ds(z * L, L)] = jnp.swapaxes(contact[:, 0].reshape(2, L, B, B), 0, 1)

    barrier = pltpu.get_barrier_semaphore()

    @pl.when(z > 0)
    def _():
        pl.semaphore_signal(barrier, inc=1, device_id={"pan": z - 1}, device_id_type=MESH)

    @pl.when(z < n - 1)
    def _():
        pl.semaphore_signal(barrier, inc=1, device_id={"pan": z + 1}, device_id_type=MESH)

    pl.semaphore_signal(barrier, inc=1, device_id={"en": other}, device_id_type=MESH)

    def target(dx):
        return lax.rem(x + dx, X) * 2 + core

    for dx in range(1, X):
        pl.semaphore_signal(barrier, inc=1, device_id={"en": target(dx)}, device_id_type=MESH)

    ends = (z > 0).astype(jnp.int32) + (z < n - 1).astype(jnp.int32)
    pl.semaphore_wait(barrier, X + ends)

    def zcopy(it, k, side):
        return pltpu.make_async_remote_copy(
            src_ref=zbuf.at[it, k], dst_ref=zbuf.at[it, k],
            send_sem=zs.at[it, side, k], recv_sem=zr.at[it, k],
            device_id={"pan": z + 1 - 2 * side}, device_id_type=MESH,
        )

    def send_own(it, b):
        k = z * L + b

        @pl.when(z < n - 1)
        def _():
            zcopy(it, k, 0).start()

        @pl.when(z > 0)
        def _():
            zcopy(it, k, 1).start()

    def cols(k):
        return pl.ds(pl.multiple_of(k * B, B), B)

    def cut(p):
        return lax.div(p * NB, max(n - 2, 1)) if n > 2 else p * 0 + NB // 2

    cut_here = cut(z)
    cut_before = cut(jnp.maximum(z - 1, 0))

    def next_copy(k):
        return pltpu.make_async_remote_copy(
            src_ref=gst.at[:, pl.ds(0, B), cols(k)], dst_ref=gnext.at[k],
            send_sem=ns.at[k], recv_sem=nr.at[k],
            device_id={"pan": z - 1}, device_id_type=MESH,
        )

    def prev_copy(k):
        return pltpu.make_async_remote_copy(
            src_ref=gst.at[:, pl.ds(rows - B, B), cols(k)], dst_ref=gprev.at[k],
            send_sem=ps.at[k], recv_sem=pr.at[k],
            device_id={"pan": z + 1}, device_id_type=MESH,
        )

    def next_sent(k):
        return jnp.logical_and(z > 0, k < cut_before)

    def prev_sent(k):
        return jnp.logical_and(z < n - 1, k >= cut_here)

    def send_edge(k):
        @pl.when(next_sent(k))
        def _():
            next_copy(k).start()

        @pl.when(prev_sent(k))
        def _():
            prev_copy(k).start()

    def absorb(it, k):
        if it == 0:
            cat = jnp.concatenate([gst[0, :, cols(k)], gst[1, :, cols(k)]], axis=1)
            hi, lo = split(cat)
            for part, ref in ((hi, rhi), (lo, rlo)):
                ref[k, :, :B, :] = part.reshape(L, B, 2 * B)
                ref[k, :, B:, :] = jnp.concatenate(
                    [-part[:, B:], part[:, :B]], axis=1
                ).reshape(L, B, 2 * B)
            left = (hi, lo)
        else:
            left = tuple(ref[k, :, :B, :].reshape(rows, 2 * B) for ref in (rhi, rlo))
        re, im = zbuf[it, k, 0], zbuf[it, k, 1]
        mixed = split(
            jnp.concatenate(
                [jnp.concatenate([re, im], axis=1), jnp.concatenate([-im, re], axis=1)], axis=0
            )
        )
        prod = split(three(nn, left, mixed))
        for j in range(L):
            right = (rhi[k, j], rlo[k, j])
            if it < ITERS - 1 or j == 0:
                got = three(nt, tuple(p[j * B:(j + 1) * B] for p in prod), right)
                dacc[j] += got
            else:
                got = three(nt, tuple(p[(j - 1) * B:(j + 1) * B] for p in prod), right)
                uacc[j - 1] += got[:B]
                dacc[j] += got[B:]
        if it == ITERS - 1:
            @pl.when(jnp.logical_and(z < n - 1, k < cut_here))
            def _():
                next_copy(k).wait_recv()
                gr, gi = gnext[k, 0], gnext[k, 1]
                right = split(
                    jnp.concatenate(
                        [jnp.concatenate([gr, gi], axis=1), jnp.concatenate([-gi, gr], axis=1)],
                        axis=0,
                    )
                )
                uacc[L - 1] += three(nt, tuple(p[rows - B:] for p in prod), right)

            @pl.when(jnp.logical_and(z > 0, k >= cut_before))
            def _():
                prev_copy(k).wait_recv()
                edge = split(jnp.concatenate([gprev[k, 0], gprev[k, 1]], axis=1))
                edge = split(three(nn, edge, mixed))
                uret[...] += three(nt, edge, (rhi[k, 0], rlo[k, 0]))

    steps = n * L
    per = -(-NB // max(steps - 2 * L, 1))

    def gather(it):
        @pl.loop(0, steps)
        def _(u):
            d = lax.div(u, L)
            b = lax.rem(u, L)

            @pl.loop(0, 2)
            def _(side):
                panel = z - d + side * 2 * d
                valid = (panel >= 0) & (panel < n) & ((d > 0) | (side == 0))
                k = panel * L + b

                @pl.when(valid)
                def _():
                    @pl.when(d > 0)
                    def _():
                        zcopy(it, k, side).wait_recv()
                        onward = z + 1 - 2 * side

                        @pl.when((onward >= 0) & (onward < n))
                        def _():
                            zcopy(it, k, side).start()

                    absorb(it, k)

            if it == 0:
                for i in range(per):
                    k = (u - 2 * L) * per + i

                    @pl.when((k >= 0) & (k < NB))
                    def _():
                        send_edge(k)

    def weight(m, target_energy, source):
        gap = shifts[m]
        hit = (source == target_energy + gap) | (source == target_energy - gap)
        return jnp.where(hit, jnp.float32(1.0), jnp.float32(0.0))

    def factor(b, target_energy, source):
        total = None
        for m in range(modes):
            col = ccol[b * B:(b + 1) * B, m:m + 1] * weight(m, target_energy, source)
            term = col * crow[b, m:m + 1, :]
            total = term if total is None else total + term
        return jnp.concatenate([total, total], axis=1)

    def sib_copy(it, b):
        return pltpu.make_async_remote_copy(
            src_ref=dbuf.at[it, b], dst_ref=sib.at[it, b],
            send_sem=ss.at[it, b], recv_sem=sr.at[it, b],
            device_id={"en": other}, device_id_type=MESH,
        )

    def x_copy(it, dx, b):
        return pltpu.make_async_remote_copy(
            src_ref=xsend.at[it, dx - 1, b], dst_ref=xrecv.at[it, dx - 1, b],
            send_sem=xs.at[it, dx - 1, b], recv_sem=xr.at[it, dx - 1, b],
            device_id={"en": target(dx)}, device_id_type=MESH,
        )

    def exchange(it, done):
        for b in range(L):
            dbuf[it, b] = dacc[b] * scale
            sib_copy(it, b).start()
        for b in range(L):
            sib_copy(it, b).wait_recv()
            for dx in range(1, X):
                to = target(dx)
                xsend[it, dx - 1, b] = (
                    factor(b, to, e) * dbuf[it, b] + factor(b, to, other) * sib[it, b]
                )
                x_copy(it, dx, b).start()
        for b in range(L):
            total = factor(b, e, e) * dbuf[it, b] + factor(b, e, other) * sib[it, b]
            for dx in range(1, X):
                x_copy(it, dx, b).wait_recv()
                total = total + xrecv[it, dx - 1, b]
            span = slice(b * B, (b + 1) * B)
            done(b, contact[0, 0, span] + total[:, :B], contact[1, 0, span] + total[:, B:])

    for b in range(L):
        send_own(0, b)
    dacc[...] = jnp.zeros_like(dacc)
    uacc[...] = jnp.zeros_like(uacc)
    uret[...] = jnp.zeros_like(uret)
    load.wait()

    for it in range(ITERS):
        gather(it)
        if it < ITERS - 1:
            def done(b, re, im):
                k = z * L + b
                zbuf[it + 1, k, 0] = re
                zbuf[it + 1, k, 1] = im
                send_own(it + 1, b)

            exchange(it, done)
            dacc[...] = jnp.zeros_like(dacc)

    back = pltpu.make_async_remote_copy(
        src_ref=uret, dst_ref=uadd, send_sem=us, recv_sem=ur,
        device_id={"pan": z - 1}, device_id_type=MESH,
    )

    @pl.when(z > 0)
    def _():
        back.start()

    def final(b, re, im):
        span = slice(b * B, (b + 1) * B)
        sigma_out[0, 0, span] = re
        sigma_out[1, 0, span] = im

    exchange(ITERS - 1, final)

    @pl.when(z < n - 1)
    def _():
        back.wait_recv()
        uacc[L - 1] += uadd[...]

    for b in range(L):
        span = slice(b * B, (b + 1) * B)
        diag_out[0, 0, span] = dbuf[ITERS - 1, b, :, :B]
        diag_out[1, 0, span] = dbuf[ITERS - 1, b, :, B:]
        upper_out[0, 0, span] = uacc[b, :, :B] * scale
        upper_out[1, 0, span] = uacc[b, :, B:] * scale

    @pl.when(z > 0)
    def _():
        back.wait_send()

    for it in range(ITERS):
        for b in range(L):
            sib_copy(it, b).wait_send()
            for dx in range(1, X):
                x_copy(it, dx, b).wait_send()

    @pl.loop(0, NB)
    def _(k):
        panel = lax.div(k, L)
        for it in range(ITERS):
            @pl.when((panel <= z) & (z < n - 1))
            def _():
                zcopy(it, k, 0).wait_send()

            @pl.when((panel >= z) & (z > 0))
            def _():
                zcopy(it, k, 1).wait_send()

        @pl.when(next_sent(k))
        def _():
            next_copy(k).wait_send()

        @pl.when(prev_sent(k))
        def _():
            prev_copy(k).wait_send()


def body(n, energies, retarded, contact, atom_kind, coupling, shifts):
    rows, columns = retarded.shape[2:]
    L = rows // B
    NB = n * L
    X = energies // 2
    kinds, modes = coupling.shape
    atoms = rows // ORB
    pan = lax.axis_index("pan")
    mine = lax.dynamic_slice_in_dim(atom_kind, pan * atoms, atoms, 0)
    per_atom = jnp.zeros((atoms, modes), jnp.float32)
    for q in range(kinds):
        per_atom = jnp.where((mine == q)[:, None], coupling[q][None, :], per_atom)
    ccol = jnp.repeat(per_atom, ORB, axis=0)
    crow = jnp.swapaxes(ccol.reshape(L, B, modes), 1, 2)
    f32, bf16 = jnp.float32, jnp.bfloat16
    out = jax.ShapeDtypeStruct(contact.shape, f32)
    vmem = pl.BlockSpec(memory_space=pltpu.VMEM)
    dma = pltpu.SemaphoreType.DMA
    far = max(X - 1, 1)
    return pl.pallas_call(
        functools.partial(kernel, n, energies, L, modes),
        out_shape=(out, out, out),
        in_specs=[
            pl.BlockSpec(memory_space=pl.ANY), vmem, vmem, vmem,
            pl.BlockSpec(memory_space=pltpu.SMEM),
        ],
        out_specs=(vmem, vmem, vmem),
        scratch_shapes=[
            pltpu.VMEM((2, rows, columns), f32),
            pltpu.VMEM((NB, L, 2 * B, 2 * B), bf16),
            pltpu.VMEM((NB, L, 2 * B, 2 * B), bf16),
            pltpu.VMEM((ITERS, NB, 2, B, B), f32),
            pltpu.VMEM((NB, 2, B, B), f32),
            pltpu.VMEM((NB, 2, B, B), f32),
            pltpu.VMEM((L, B, 2 * B), f32),
            pltpu.VMEM((L, B, 2 * B), f32),
            pltpu.VMEM((B, 2 * B), f32),
            pltpu.VMEM((B, 2 * B), f32),
            pltpu.VMEM((ITERS, L, B, 2 * B), f32),
            pltpu.VMEM((ITERS, L, B, 2 * B), f32),
            pltpu.VMEM((ITERS, far, L, B, 2 * B), f32),
            pltpu.VMEM((ITERS, far, L, B, 2 * B), f32),
            dma,
            dma((ITERS, 2, NB)), dma((ITERS, NB)),
            dma((NB,)), dma((NB,)), dma((NB,)), dma((NB,)),
            dma, dma,
            dma((ITERS, L)), dma((ITERS, L)),
            dma((ITERS, far, L)), dma((ITERS, far, L)),
        ],
        compiler_params=pltpu.CompilerParams(
            collective_id=0, has_side_effects=True, vmem_limit_bytes=58 * 2**20
        ),
        cost_estimate=pl.CostEstimate(
            flops=2 * 3 * 20 * rows * columns * B, bytes_accessed=8 * rows * columns,
            transcendentals=0,
        ),
    )(retarded, contact, ccol, crow, shifts)


def solution(mesh):
    shape = dict(mesh.shape)
    spec = P(None, ("grp", "en"), "pan", None)
    return jax.shard_map(
        functools.partial(body, shape["pan"], shape["en"]),
        mesh=mesh,
        in_specs=(spec, spec, P(), P(), P()),
        out_specs=(spec, spec, spec),
        check_vma=False,
    )
```

profile of v0, /device:TPU:0, one launch (start us, length us, event | category | flops | bytes accessed | tf_op | source)
XLA Modules:
  0.0 127.2 jit_solution(17252582367390173257)
XLA Ops:
  0.6 0.8 broadcast_compare_fusion.3
  1.4 0.8 slice_bitcast_fusion.3
  2.2 0.1 select_select_fusion
  2.3 0.1 copy.10
  2.4 0.1 broadcast_in_dim.77
  2.5 0.1 reshape_reshape.3
  2.6 0.6 copy.12
  3.2 0.7 broadcast_bitcast_fusion.ccol
  3.9 117.6 %shard_map.76 = (f32[2,1,512,128]{3,2,1,0:T(8,128)}, f32[2,1,512,128]{3,2,1,0:T(8,128)}, f32[2,1,512,128]{3,2,1,0:T(8,128)}) custom-call(f32[2,1,512,2048]{3,2,1,0:T(8,128)} %green.1, f32[2,1,512,128]{3,2,1,0:T(8,128)} %contact.1, f32[512,3]{1,0:T(8,128)} %broadcast_bitcast_fusion.ccol, f32[4,3,128]{2,1,0:T(4,128)} %bitcast.15, s32[3]{0:T(128)} %shifts.1), custom_call_target="tpu_custom_call" | custom-call | flops 16106127360 | bytes 8388608 | tf_op jit(solution)/shard_map/pallas_call | solution.py:360
  121.6 1.9 %copy.16 = f32[2,1,512,128]{3,2,1,0:T(8,128)} copy(f32[2,1,512,128]{3,2,1,0:T(8,128)} %get-tuple-element.15) | data formatting | bytes 1048576
  123.5 1.9 %copy.17 = f32[2,1,512,128]{3,2,1,0:T(8,128)} copy(f32[2,1,512,128]{3,2,1,0:T(8,128)} %get-tuple-element.16) | data formatting | bytes 1048576
  125.3 1.9 %copy.18 = f32[2,1,512,128]{3,2,1,0:T(8,128)} copy(f32[2,1,512,128]{3,2,1,0:T(8,128)} %get-tuple-element.17) | data formatting | bytes 1048576
  (1 shorter events, 0.0 us)
where the time goes:
time: 128 us; the launch traced here: 127 us
  Pallas kernels  118 us (92%)
  local copies, waits for them, and re-layouts  8.05 us (6%)
    pallas_call x1, Pallas kernels, body(): pl.pallas_call(functools.partial(kernel, n, energies, L, modes), out_shap...  118 us
    unnamed x4, local copies, waits for them, and re-layouts  5.7 us

commit v1 on v0

--- a/solution.py
+++ b/solution.py
@@ -31,12 +31,20 @@
     return f(a[0], b[0]) + (f(a[1], b[0]) + f(a[0], b[1]))
 
 
+def mix(re, im):
+    return split(
+        jnp.concatenate(
+            [jnp.concatenate([re, im], axis=1), jnp.concatenate([-im, re], axis=1)], axis=0
+        )
+    )
+
+
 def kernel(
     n, energies, L, modes,
-    green, contact, ccol, crow, shifts,
+    green, contact, atom_kind, coupling, shifts,
     diag_out, upper_out, sigma_out,
-    gst, rhi, rlo, zbuf, gnext, gprev, dacc, uacc, uret, uadd, dbuf, sib, xsend, xrecv,
-    gsem, zs, zr, ns, nr, ps, pr, us, ur, ss, sr, xs, xr,
+    gst, rhi, rlo, fac, phi, plo, zbuf, gnext, gprev, dacc, uacc, uret, uadd, dbuf, sib, xsend, xrecv,
+    gsem, csem, zs, zr, ns, nr, ps, pr, us, ur, ss, sr, xs, xr,
 ):
     NB = n * L
     rows = L * B
@@ -50,7 +58,14 @@
 
     load = pltpu.make_async_copy(green.at[:, 0], gst, gsem)
     load.start()
-    zbuf[0, pl.ds(z * L, L)] = jnp.swapaxes(contact[:, 0].reshape(2, L, B, B), 0, 1)
+    own = [
+        pltpu.make_async_copy(
+            contact.at[:, 0, pl.ds(b * B, B)], zbuf.at[0, z * L + b], csem.at[b]
+        )
+        for b in range(L)
+    ]
+    for copy in own:
+        copy.start()
 
     barrier = pltpu.get_barrier_semaphore()
 
@@ -82,6 +97,8 @@
 
     def send_own(it, b):
         k = z * L + b
+        if it == 0:
+            own[b].wait()
 
         @pl.when(z < n - 1)
         def _():
@@ -120,14 +137,30 @@
     def prev_sent(k):
         return jnp.logical_and(z < n - 1, k >= cut_here)
 
-    def send_edge(k):
-        @pl.when(next_sent(k))
-        def _():
-            next_copy(k).start()
-
-        @pl.when(prev_sent(k))
-        def _():
-            prev_copy(k).start()
+    at_end = ((z == 0) | (z == n - 1)).astype(jnp.int32)
+
+    def paced(it, u):
+        fast = lax.div(3 * jnp.maximum(u + 1 - 2 * L, 0), 2)
+        slow = jnp.maximum(u + 1 - (n - 1) * L, 0)
+        first = at_end * fast + (1 - at_end) * slow
+        if it == 0:
+            return jnp.minimum(first, NB)
+        most = at_end * lax.div(3 * (n - 2) * L, 2) + (1 - at_end) * L
+        later = at_end * jnp.maximum(u + 1 - L, 0) + (1 - at_end) * jnp.maximum(u + 1 - 2 * L, 0)
+        return jnp.minimum(most + later, NB)
+
+    def send_edge(begin, end):
+        @pl.loop(begin, end)
+        def _(i):
+            right = cut_here + i
+
+            @pl.when((z > 0) & (i < cut_before))
+            def _():
+                next_copy(i).start()
+
+            @pl.when((z < n - 1) & (right < NB))
+            def _():
+                prev_copy(right).start()
 
     def absorb(it, k):
         if it == 0:
@@ -141,12 +174,7 @@
             left = (hi, lo)
         else:
             left = tuple(ref[k, :, :B, :].reshape(rows, 2 * B) for ref in (rhi, rlo))
-        re, im = zbuf[it, k, 0], zbuf[it, k, 1]
-        mixed = split(
-            jnp.concatenate(
-                [jnp.concatenate([re, im], axis=1), jnp.concatenate([-im, re], axis=1)], axis=0
-            )
-        )
+        mixed = mix(zbuf[it, k, 0], zbuf[it, k, 1])
         prod = split(three(nn, left, mixed))
         for j in range(L):
             right = (rhi[k, j], rlo[k, j])
@@ -158,7 +186,13 @@
                 uacc[j - 1] += got[:B]
                 dacc[j] += got[B:]
         if it == ITERS - 1:
-            @pl.when(jnp.logical_and(z < n - 1, k < cut_here))
+            phi[k] = prod[0][rows - B:]
+            plo[k] = prod[1][rows - B:]
+
+    def edges():
+        @pl.loop(0, NB)
+        def _(k):
+            @pl.when((z < n - 1) & (k < cut_here))
             def _():
                 next_copy(k).wait_recv()
                 gr, gi = gnext[k, 0], gnext[k, 1]
@@ -168,17 +202,16 @@
                         axis=0,
                     )
                 )
-                uacc[L - 1] += three(nt, tuple(p[rows - B:] for p in prod), right)
-
-            @pl.when(jnp.logical_and(z > 0, k >= cut_before))
+                uacc[L - 1] += three(nt, (phi[k], plo[k]), right)
+
+            @pl.when((z > 0) & (k >= cut_before))
             def _():
                 prev_copy(k).wait_recv()
                 edge = split(jnp.concatenate([gprev[k, 0], gprev[k, 1]], axis=1))
-                edge = split(three(nn, edge, mixed))
+                edge = split(three(nn, edge, mix(zbuf[ITERS - 1, k, 0], zbuf[ITERS - 1, k, 1])))
                 uret[...] += three(nt, edge, (rhi[k, 0], rlo[k, 0]))
 
     steps = n * L
-    per = -(-NB // max(steps - 2 * L, 1))
 
     def gather(it):
         @pl.loop(0, steps)
@@ -205,13 +238,13 @@
 
                     absorb(it, k)
 
-            if it == 0:
-                for i in range(per):
-                    k = (u - 2 * L) * per + i
-
-                    @pl.when((k >= 0) & (k < NB))
-                    def _():
-                        send_edge(k)
+            begin = paced(it, u - 1)
+            if it == ITERS - 1:
+                begin = jnp.where(u == 0, paced(0, steps - 1), begin)
+            send_edge(begin, paced(it, u))
+
+        if it == ITERS - 1:
+            send_edge(paced(it, steps - 1), NB)
 
     def weight(m, target_energy, source):
         gap = shifts[m]
@@ -219,12 +252,23 @@
         return jnp.where(hit, jnp.float32(1.0), jnp.float32(0.0))
 
     def factor(b, target_energy, source):
-        total = None
-        for m in range(modes):
-            col = ccol[b * B:(b + 1) * B, m:m + 1] * weight(m, target_energy, source)
-            term = col * crow[b, m:m + 1, :]
-            total = term if total is None else total + term
+        total = sum(fac[m, b] * weight(m, target_energy, source) for m in range(modes))
         return jnp.concatenate([total, total], axis=1)
+
+    def make_factor():
+        per_block = B // ORB
+        lane_atom = lax.div(lax.broadcasted_iota(jnp.int32, (ORB, B), 1), ORB)
+
+        @pl.loop(0, L)
+        def _(b):
+            kinds = [atom_kind[(z * L + b) * per_block + a] for a in range(per_block)]
+            for m in range(modes):
+                values = [coupling[kind, m] for kind in kinds]
+                row = jnp.zeros((ORB, B), jnp.float32)
+                for a, value in enumerate(values):
+                    row = jnp.where(lane_atom == a, value, row)
+                for a, value in enumerate(values):
+                    fac[m, b, a * ORB:(a + 1) * ORB, :] = value * row
 
     def sib_copy(it, b):
         return pltpu.make_async_remote_copy(
@@ -240,7 +284,7 @@
             device_id={"en": target(dx)}, device_id_type=MESH,
         )
 
-    def exchange(it, done):
+    def exchange(it, done, between):
         for b in range(L):
             dbuf[it, b] = dacc[b] * scale
             sib_copy(it, b).start()
@@ -252,19 +296,21 @@
                     factor(b, to, e) * dbuf[it, b] + factor(b, to, other) * sib[it, b]
                 )
                 x_copy(it, dx, b).start()
+        between()
         for b in range(L):
             total = factor(b, e, e) * dbuf[it, b] + factor(b, e, other) * sib[it, b]
             for dx in range(1, X):
                 x_copy(it, dx, b).wait_recv()
                 total = total + xrecv[it, dx - 1, b]
-            span = slice(b * B, (b + 1) * B)
-            done(b, contact[0, 0, span] + total[:, :B], contact[1, 0, span] + total[:, B:])
+            k = z * L + b
+            done(b, zbuf[0, k, 0] + total[:, :B], zbuf[0, k, 1] + total[:, B:])
 
     for b in range(L):
         send_own(0, b)
     dacc[...] = jnp.zeros_like(dacc)
     uacc[...] = jnp.zeros_like(uacc)
     uret[...] = jnp.zeros_like(uret)
+    make_factor()
     load.wait()
 
     for it in range(ITERS):
@@ -276,7 +322,7 @@
                 zbuf[it + 1, k, 1] = im
                 send_own(it + 1, b)
 
-            exchange(it, done)
+            exchange(it, done, lambda: None)
             dacc[...] = jnp.zeros_like(dacc)
 
     back = pltpu.make_async_remote_copy(
@@ -284,16 +330,19 @@
         device_id={"pan": z - 1}, device_id_type=MESH,
     )
 
-    @pl.when(z > 0)
-    def _():
-        back.start()
+    def between():
+        edges()
+
+        @pl.when(z > 0)
+        def _():
+            back.start()
 
     def final(b, re, im):
         span = slice(b * B, (b + 1) * B)
         sigma_out[0, 0, span] = re
         sigma_out[1, 0, span] = im
 
-    exchange(ITERS - 1, final)
+    exchange(ITERS - 1, final, between)
 
     @pl.when(z < n - 1)
     def _():
@@ -338,37 +387,39 @@
             prev_copy(k).wait_send()
 
 
+def place(diag, upper, sigma, diag_out, upper_out, sigma_out):
+    diag_out[...] = diag[...]
+    upper_out[...] = upper[...]
+    sigma_out[...] = sigma[...]
+
+
 def body(n, energies, retarded, contact, atom_kind, coupling, shifts):
     rows, columns = retarded.shape[2:]
     L = rows // B
     NB = n * L
     X = energies // 2
-    kinds, modes = coupling.shape
-    atoms = rows // ORB
-    pan = lax.axis_index("pan")
-    mine = lax.dynamic_slice_in_dim(atom_kind, pan * atoms, atoms, 0)
-    per_atom = jnp.zeros((atoms, modes), jnp.float32)
-    for q in range(kinds):
-        per_atom = jnp.where((mine == q)[:, None], coupling[q][None, :], per_atom)
-    ccol = jnp.repeat(per_atom, ORB, axis=0)
-    crow = jnp.swapaxes(ccol.reshape(L, B, modes), 1, 2)
+    modes = coupling.shape[1]
     f32, bf16 = jnp.float32, jnp.bfloat16
     out = jax.ShapeDtypeStruct(contact.shape, f32)
     vmem = pl.BlockSpec(memory_space=pltpu.VMEM)
+    anywhere = pl.BlockSpec(memory_space=pl.ANY)
+    scalars = pl.BlockSpec(memory_space=pltpu.SMEM)
     dma = pltpu.SemaphoreType.DMA
     far = max(X - 1, 1)
-    return pl.pallas_call(
+    results = pl.pallas_call(
         functools.partial(kernel, n, energies, L, modes),
         out_shape=(out, out, out),
         in_specs=[
-            pl.BlockSpec(memory_space=pl.ANY), vmem, vmem, vmem,
-            pl.BlockSpec(memory_space=pltpu.SMEM),
+            anywhere, anywhere, scalars, scalars, scalars,
         ],
         out_specs=(vmem, vmem, vmem),
         scratch_shapes=[
             pltpu.VMEM((2, rows, columns), f32),
             pltpu.VMEM((NB, L, 2 * B, 2 * B), bf16),
             pltpu.VMEM((NB, L, 2 * B, 2 * B), bf16),
+            pltpu.VMEM((modes, L, B, B), f32),
+            pltpu.VMEM((NB, B, 2 * B), bf16),
+            pltpu.VMEM((NB, B, 2 * B), bf16),
             pltpu.VMEM((ITERS, NB, 2, B, B), f32),
             pltpu.VMEM((NB, 2, B, B), f32),
             pltpu.VMEM((NB, 2, B, B), f32),
@@ -380,7 +431,7 @@
             pltpu.VMEM((ITERS, L, B, 2 * B), f32),
             pltpu.VMEM((ITERS, far, L, B, 2 * B), f32),
             pltpu.VMEM((ITERS, far, L, B, 2 * B), f32),
-            dma,
+            dma, dma((L,)),
             dma((ITERS, 2, NB)), dma((ITERS, NB)),
             dma((NB,)), dma((NB,)), dma((NB,)), dma((NB,)),
             dma, dma,
@@ -394,7 +445,13 @@
             flops=2 * 3 * 20 * rows * columns * B, bytes_accessed=8 * rows * columns,
             transcendentals=0,
         ),
-    )(retarded, contact, ccol, crow, shifts)
+    )(retarded, contact, atom_kind, coupling, shifts)
+    return pl.pallas_call(
+        place,
+        out_shape=(out, out, out),
+        in_specs=[vmem] * 3,
+        out_specs=(vmem,) * 3,
+    )(*results)
 
 
 def solution(mesh):

time: 128 us -> 109 us (0.85)
  Pallas kernels: 118 us -> 108 us
  local copies, waits for them, and re-layouts: 8.05 us -> 0 us
    pallas_call x1, Pallas kernels: 118 us -> 105 us  [body(): pl.pallas_call(functools.partial(kernel, n, energies, L, modes), out_shap...]
    unnamed x4 -> x0, local copies, waits for them, and re-layouts: 5.7 us -> none
    pallas_call x0 -> x1, Pallas kernels: none -> 2.53 us  [body(): pl.pallas_call(place, out_shape=(out, out, out), in_specs=[vmem] * 3, out...]
where the time goes in v1:
time: 109 us
  Pallas kernels  108 us (99%)
    pallas_call x1, Pallas kernels, body(): pl.pallas_call(functools.partial(kernel, n, energies, L, modes), out_shap...  105 us
    pallas_call x1, Pallas kernels, body(): pl.pallas_call(place, out_shape=(out, out, out), in_specs=[vmem] * 3, out...  2.53 us

profile of v1, /device:TPU:0, one launch (start us, length us, event | category | flops | bytes accessed | tf_op | source)
XLA Modules:
  0.0 108.7 jit_solution(12624544561322024385)
XLA Ops:
  0.6 105.5 %shard_map.76 = (f32[2,1,512,128]{3,2,1,0:T(8,128)}, f32[2,1,512,128]{3,2,1,0:T(8,128)}, f32[2,1,512,128]{3,2,1,0:T(8,128)}) custom-call(f32[2,1,512,2048]{3,2,1,0:T(8,128)} %green.1, f32[2,1,512,128]{3,2,1,0:T(8,128)} %contact.1, s32[256]{0:T(256)} %atom_kind.1, f32[4,3]{1,0:T(4,128)} %coupling.1, s32[3]{0:T(128)} %shifts.1), custom_call_target="tpu_custom_call" | custom-call | flops 16106127360 | bytes 8388608 | tf_op jit(solution)/shard_map/pallas_call | solution.py:409
  106.1 2.5 %shard_map.77 = (f32[2,1,512,128]{3,2,1,0:T(8,128)}, f32[2,1,512,128]{3,2,1,0:T(8,128)}, f32[2,1,512,128]{3,2,1,0:T(8,128)}) custom-call(f32[2,1,512,128]{3,2,1,0:T(8,128)} %get-tuple-element.6.diag, f32[2,1,512,128]{3,2,1,0:T(8,128)} %get-tuple-element.7.upper, f32[2,1,512,128]{3,2,1,0:T(8,128)} %get-tuple-element.8.sigma), custom_call_target="tpu_custom_call" | custom-call | tf_op jit(solution)/shard_map/pallas_call | solution.py:449

commit v2 on v1

--- a/solution.py
+++ b/solution.py
@@ -44,7 +44,7 @@
     green, contact, atom_kind, coupling, shifts,
     diag_out, upper_out, sigma_out,
     gst, rhi, rlo, fac, phi, plo, zbuf, gnext, gprev, dacc, uacc, uret, uadd, dbuf, sib, xsend, xrecv,
-    gsem, csem, zs, zr, ns, nr, ps, pr, us, ur, ss, sr, xs, xr,
+    gsem, csem, osem, zs, zr, ns, nr, ps, pr, us, ur, ss, sr, xs, xr,
 ):
     NB = n * L
     rows = L * B
@@ -139,15 +139,15 @@
 
     at_end = ((z == 0) | (z == n - 1)).astype(jnp.int32)
 
+    early = at_end * lax.div(3 * (n - 2) * L, 2) + (1 - at_end) * L
+
     def paced(it, u):
-        fast = lax.div(3 * jnp.maximum(u + 1 - 2 * L, 0), 2)
+        fast = jnp.minimum(jnp.maximum(u + 1 - L, 0), early)
         slow = jnp.maximum(u + 1 - (n - 1) * L, 0)
         first = at_end * fast + (1 - at_end) * slow
         if it == 0:
             return jnp.minimum(first, NB)
-        most = at_end * lax.div(3 * (n - 2) * L, 2) + (1 - at_end) * L
-        later = at_end * jnp.maximum(u + 1 - L, 0) + (1 - at_end) * jnp.maximum(u + 1 - 2 * L, 0)
-        return jnp.minimum(most + later, NB)
+        return jnp.minimum(early + at_end * jnp.maximum(u + 1 - L, 0) + (1 - at_end) * jnp.maximum(u + 1 - 2 * L, 0), NB)
 
     def send_edge(begin, end):
         @pl.loop(begin, end)
@@ -189,7 +189,17 @@
             phi[k] = prod[0][rows - B:]
             plo[k] = prod[1][rows - B:]
 
-    def edges():
+    def edges_before():
+        @pl.loop(0, NB)
+        def _(k):
+            @pl.when((z > 0) & (k >= cut_before))
+            def _():
+                prev_copy(k).wait_recv()
+                edge = split(jnp.concatenate([gprev[k, 0], gprev[k, 1]], axis=1))
+                edge = split(three(nn, edge, mix(zbuf[ITERS - 1, k, 0], zbuf[ITERS - 1, k, 1])))
+                uret[...] += three(nt, edge, (rhi[k, 0], rlo[k, 0]))
+
+    def edges_after():
         @pl.loop(0, NB)
         def _(k):
             @pl.when((z < n - 1) & (k < cut_here))
@@ -203,13 +213,6 @@
                     )
                 )
                 uacc[L - 1] += three(nt, (phi[k], plo[k]), right)
-
-            @pl.when((z > 0) & (k >= cut_before))
-            def _():
-                prev_copy(k).wait_recv()
-                edge = split(jnp.concatenate([gprev[k, 0], gprev[k, 1]], axis=1))
-                edge = split(three(nn, edge, mix(zbuf[ITERS - 1, k, 0], zbuf[ITERS - 1, k, 1])))
-                uret[...] += three(nt, edge, (rhi[k, 0], rlo[k, 0]))
 
     steps = n * L
 
@@ -325,22 +328,40 @@
             exchange(it, done, lambda: None)
             dacc[...] = jnp.zeros_like(dacc)
 
+    puts = []
+
+    def put(out, which, block, b):
+        for part in range(2):
+            copy = pltpu.make_async_copy(
+                block.at[:, pl.ds(part * B, B)], out.at[part, 0, pl.ds(b * B, B)],
+                osem.at[which, b, part],
+            )
+            copy.start()
+            puts.append(copy)
+
     back = pltpu.make_async_remote_copy(
         src_ref=uret, dst_ref=uadd, send_sem=us, recv_sem=ur,
         device_id={"pan": z - 1}, device_id_type=MESH,
     )
 
     def between():
-        edges()
+        for b in range(L):
+            put(diag_out, 0, dbuf.at[ITERS - 1, b], b)
+        for b in range(L - 1):
+            uacc[b] = uacc[b] * scale
+            put(upper_out, 1, uacc.at[b], b)
+        edges_before()
 
         @pl.when(z > 0)
         def _():
             back.start()
 
+        edges_after()
+
     def final(b, re, im):
-        span = slice(b * B, (b + 1) * B)
-        sigma_out[0, 0, span] = re
-        sigma_out[1, 0, span] = im
+        dacc[b, :, :B] = re
+        dacc[b, :, B:] = im
+        put(sigma_out, 2, dacc.at[b], b)
 
     exchange(ITERS - 1, final, between)
 
@@ -349,12 +370,8 @@
         back.wait_recv()
         uacc[L - 1] += uadd[...]
 
-    for b in range(L):
-        span = slice(b * B, (b + 1) * B)
-        diag_out[0, 0, span] = dbuf[ITERS - 1, b, :, :B]
-        diag_out[1, 0, span] = dbuf[ITERS - 1, b, :, B:]
-        upper_out[0, 0, span] = uacc[b, :, :B] * scale
-        upper_out[1, 0, span] = uacc[b, :, B:] * scale
+    uacc[L - 1] = uacc[L - 1] * scale
+    put(upper_out, 1, uacc.at[L - 1], L - 1)
 
     @pl.when(z > 0)
     def _():
@@ -385,6 +402,9 @@
         @pl.when(prev_sent(k))
         def _():
             prev_copy(k).wait_send()
+
+    for copy in puts:
+        copy.wait()
 
 
 def place(diag, upper, sigma, diag_out, upper_out, sigma_out):
@@ -412,7 +432,7 @@
         in_specs=[
             anywhere, anywhere, scalars, scalars, scalars,
         ],
-        out_specs=(vmem, vmem, vmem),
+        out_specs=(anywhere,) * 3,
         scratch_shapes=[
             pltpu.VMEM((2, rows, columns), f32),
             pltpu.VMEM((NB, L, 2 * B, 2 * B), bf16),
@@ -431,7 +451,7 @@
             pltpu.VMEM((ITERS, L, B, 2 * B), f32),
             pltpu.VMEM((ITERS, far, L, B, 2 * B), f32),
             pltpu.VMEM((ITERS, far, L, B, 2 * B), f32),
-            dma, dma((L,)),
+            dma, dma((L,)), dma((3, L, 2)),
             dma((ITERS, 2, NB)), dma((ITERS, NB)),
             dma((NB,)), dma((NB,)), dma((NB,)), dma((NB,)),
             dma, dma,

time: 109 us -> 102 us (0.936)
  Pallas kernels: 108 us -> 101 us
    pallas_call x1, Pallas kernels: 105 us -> 98.2 us  [body(): pl.pallas_call(functools.partial(kernel, n, energies, L, modes), out_shap...]
where the time goes in v2:
time: 102 us; the launch traced here: 101 us
  Pallas kernels  101 us (99%)
    pallas_call x1, Pallas kernels, body(): pl.pallas_call(functools.partial(kernel, n, energies, L, modes), out_shap...  98.2 us
    pallas_call x1, Pallas kernels, body(): pl.pallas_call(place, out_shape=(out, out, out), in_specs=[vmem] * 3, out...  2.53 us

profile of v2, /device:TPU:0, one launch (start us, length us, event | category | flops | bytes accessed | tf_op | source)
XLA Modules:
  0.0 101.4 jit_solution(17086196273481288027)
XLA Ops:
  0.6 98.2 %shard_map.76 = (f32[2,1,512,128]{3,2,1,0:T(8,128)}, f32[2,1,512,128]{3,2,1,0:T(8,128)}, f32[2,1,512,128]{3,2,1,0:T(8,128)}) custom-call(f32[2,1,512,2048]{3,2,1,0:T(8,128)} %green.1, f32[2,1,512,128]{3,2,1,0:T(8,128)} %contact.1, s32[256]{0:T(256)} %atom_kind.1, f32[4,3]{1,0:T(4,128)} %coupling.1, s32[3]{0:T(128)} %shifts.1), custom_call_target="tpu_custom_call" | custom-call | flops 16106127360 | bytes 8388608 | tf_op jit(solution)/shard_map/pallas_call | solution.py:429
  98.9 2.5 %shard_map.77 = (f32[2,1,512,128]{3,2,1,0:T(8,128)}, f32[2,1,512,128]{3,2,1,0:T(8,128)}, f32[2,1,512,128]{3,2,1,0:T(8,128)}) custom-call(f32[2,1,512,128]{3,2,1,0:T(8,128)} %get-tuple-element.6.diag, f32[2,1,512,128]{3,2,1,0:T(8,128)} %get-tuple-element.7.upper, f32[2,1,512,128]{3,2,1,0:T(8,128)} %get-tuple-element.8.sigma), custom_call_target="tpu_custom_call" | custom-call | tf_op jit(solution)/shard_map/pallas_call | solution.py:469
